TPU v7x, 128 devices: a whole 4x4x4 slice. The times are simulated.
128 devices in a mesh: ingest: 8 (over x, core), list: 16 (over y, z).
Axes of the slice: x: 4, y: 4, z: 4, core: 2. Of those that a mesh axis runs over, the one named last changes fastest.
Arguments:
- vectors: bfloat16 [393216, 768], P(('ingest', 'list')), may hold values from -6 to 6
- list_ids: int32 [1536], P(('ingest', 'list')), may hold values from 0 to 65535, as said below
- code_ids: int32 [393216, 96], P(('ingest', 'list')), may hold values from 0 to 255
- block_counts: int32 [128, 16], P(('ingest', 'list')), may hold values from 0 to 2, as said below
- centroids: bfloat16 [65536, 768], P('list'), may hold values from -6 to 6
- rotation: bfloat16 [768, 768], replicated, may hold values from -0.21875 to 0.21875
Outputs:
- stored_rows: bfloat16 [1048576, 768], P(('ingest', 'list'))
- codebook_sums: float32 [256, 768], P(('ingest', 'list'))
- code_counts: float32 [256, 96], P(('ingest', 'list'))
Inputs may be any that keep to these rules, and one draw needn't show every extreme that they name: `list_ids`: on each device at most 2 blocks have lists of one owner (owner = id // 4096); on each index of ingest one owner has exactly 2 blocks of every device of that index. `block_counts`: entry [d, o] is a send allowance: at most the number of blocks of device d whose list has owner o; on each index of ingest, for the owner that has 2 blocks of every device of that index, the entry is 2 on every such device.
All inputs are finite; a program needn't handle non-finite values.
Results may differ from a plain program's by a relative error of at most 0.0051.
Values may be sent and summed in bfloat16 or wider, within the bound.
A program may use at most 128 MiB of HBM per device.

v0:
```python
import math

import jax
import jax.numpy as jnp
from jax import lax
from jax.sharding import PartitionSpec as P

M = 96
DSUB = 8
KS = 256
CAP = 2


def codebook_terms(encoded, code_rows, keep_rows):
    row_count = encoded.shape[0]
    model_width = encoded.shape[1]
    step_rows = math.gcd(row_count, 512)
    turns = row_count // step_rows
    codeword = jnp.arange(KS, dtype=jnp.int32)
    ones_column = jnp.ones((step_rows,), jnp.bfloat16)

    def accumulate(carry, index):
        start = index * step_rows
        rows_here = lax.dynamic_slice_in_dim(encoded, start, step_rows, 0).reshape(
            step_rows, M, DSUB
        )
        codes_here = lax.dynamic_slice_in_dim(code_rows, start, step_rows, 0)
        keep_here = lax.dynamic_slice_in_dim(keep_rows, start, step_rows, 0)
        selector = (
            (codes_here[:, :, None] == codeword[None, None, :]) & keep_here[:, None, None]
        ).astype(jnp.bfloat16)
        sums_here = jnp.einsum(
            "rmk,rme->kme", selector, rows_here, preferred_element_type=jnp.float32
        )
        counts_here = jnp.einsum(
            "rmk,r->km", selector, ones_column, preferred_element_type=jnp.float32
        )
        return ((carry[0] + sums_here.reshape(KS, model_width), carry[1] + counts_here), None)

    start_totals = (jnp.zeros((KS, model_width), jnp.float32), jnp.zeros((KS, M), jnp.float32))
    totals, unused = lax.scan(accumulate, start_totals, jnp.arange(turns, dtype=jnp.int32))
    return totals


def shards(vectors, list_ids, code_ids, block_counts, centroids, rotation):
    list_count = lax.axis_size("list")
    block_count = list_ids.shape[0]
    block_rows = vectors.shape[0] // block_count
    model_width = vectors.shape[1]
    lists_here = centroids.shape[0]
    owner_index = list_ids // lists_here
    local_list = list_ids - owner_index * lists_here
    onehot = (owner_index[:, None] == jnp.arange(list_count, dtype=jnp.int32)[None, :]).astype(
        jnp.int32
    )
    block_rank = jnp.sum(jnp.cumsum(onehot, axis=0) * onehot, axis=1) - 1
    count_limit = jnp.sum(onehot * block_counts, axis=1)
    kept_mask = block_rank < count_limit
    slot_index = owner_index * CAP + block_rank
    selected = kept_mask[None, :] & (
        slot_index[None, :] == jnp.arange(list_count * CAP, dtype=jnp.int32)[:, None]
    )
    source_block = jnp.sum(
        selected.astype(jnp.int32) * jnp.arange(block_count, dtype=jnp.int32)[None, :], axis=1
    )
    filled = jnp.any(selected, axis=1)
    vector_blocks = vectors.reshape(block_count, block_rows * model_width)
    outgoing = jnp.where(filled[:, None], vector_blocks[source_block], jnp.zeros((), jnp.bfloat16))
    outgoing = outgoing.reshape(list_count, CAP * block_rows, model_width)
    code_blocks = code_ids.reshape(block_count, block_rows * M)
    outgoing_codes = jnp.where(filled[:, None], code_blocks[source_block], 0).reshape(
        list_count, CAP * block_rows, M
    )
    outgoing_lists = jnp.where(filled, local_list[source_block], -1).reshape(list_count, CAP)
    arrived = lax.all_to_all(outgoing, "list", split_axis=0, concat_axis=0, tiled=True)
    arrived_codes, arrived_lists = (
        lax.all_to_all(outgoing_codes, "list", split_axis=0, concat_axis=0, tiled=True),
        lax.all_to_all(outgoing_lists, "list", split_axis=0, concat_axis=0, tiled=True),
    )
    slot_used = arrived_lists >= 0
    centre_rows = centroids[jnp.maximum(arrived_lists, 0)].astype(jnp.float32)
    residual = (
        arrived.reshape(list_count, CAP, block_rows, model_width).astype(jnp.float32)
        - centre_rows[:, :, None, :]
    ).astype(jnp.bfloat16)
    rotated = jnp.dot(
        residual.reshape(list_count * CAP * block_rows, model_width),
        rotation,
        preferred_element_type=jnp.float32,
    )
    encoded = rotated.astype(jnp.bfloat16)
    keep_rows = jnp.repeat(slot_used.reshape(list_count * CAP), block_rows)
    code_sums, code_totals = codebook_terms(
        encoded, arrived_codes.reshape(list_count * CAP * block_rows, M), keep_rows
    )
    stored_rows = jnp.where(keep_rows[:, None], encoded, jnp.zeros((), jnp.bfloat16))
    sum_share, count_share = (
        lax.psum_scatter(code_sums, ("ingest", "list"), scatter_dimension=0, tiled=True),
        lax.psum_scatter(code_totals, ("ingest", "list"), scatter_dimension=0, tiled=True),
    )
    return (stored_rows, sum_share, count_share)


def solution(mesh):
    in_specs = (
        P(("ingest", "list"), None),
        P(("ingest", "list")),
        P(("ingest", "list"), None),
        P(("ingest", "list"), None),
        P("list", None),
        P(),
    )
    out_specs = (
        P(("ingest", "list"), None),
        P(("ingest", "list"), None),
        P(("ingest", "list"), None),
    )
    return jax.shard_map(shards, mesh=mesh, in_specs=in_specs, out_specs=out_specs, check_vma=False)
```

profile of v0, /device:TPU:0, one launch (start us, length us, event | category | flops | bytes accessed | tf_op | source)
XLA Modules:
  0.0 932.0 jit_solution(7701838941661450742)
XLA Ops:
  10.5 8.1 all-to-all-start
  18.7 6.4 reshape.108
  25.2 5.9 fusion.25
  31.0 14.9 %gather_fusion.3 = bf16[32,98304]{1,0:T(8,128)(2,1)} fusion(bf16[12,98304]{1,0:T(8,128)(2,1)} %get-tuple-element.129, s32[1024]{0:T(1024)S(1)} %pad_clamp_fusion.1), kind=kCustom, calls=%fused_computation.3 | custom fusion | bytes 12583040 | tf_op jit(solution)/shard_map/gather | solution.py:68
  62.9 14.8 %gather_fusion.4 = bf16[32,98304]{1,0:T(8,128)(2,1)} fusion(bf16[12,98304]{1,0:T(8,128)(2,1)} %get-tuple-element.130, s32[1024]{0:T(1024)S(1)} %pad_clamp_fusion.1), kind=kCustom, calls=%fused_computation.4 | custom fusion | bytes 12583040 | tf_op jit(solution)/shard_map/gather | solution.py:68
  77.6 5.3 copy.30
  82.9 7.5 all-to-all-start.2
  90.4 13.2 %pad_maximum_fusion = bf16[32,196608]{1,0:T(8,128)(2,1)} fusion(bf16[32,98304]{1,0:T(8,128)(2,1)} %gather_fusion.4, bf16[32,98304]{1,0:T(8,128)(2,1)} %gather_fusion.3), kind=kLoop, calls=%fused_computation.25 | loop fusion | flops 25165824 | bytes 25165824
  103.6 12.0 %gather.18 = bf16[16,512,768]{2,1,0:T(8,128)(2,1)} reshape(bf16[32,196608]{1,0:T(8,128)(2,1)} %pad_maximum_fusion) | data formatting | bytes 25165824 | tf_op jit(solution)/shard_map/gather | solution.py:68
  115.6 10.9 %broadcast_select_fusion.1 = bf16[16,512,768]{2,1,0:T(8,128)(2,1)} fusion(bf16[16,512,768]{2,1,0:T(8,128)(2,1)} %gather.18, pred[16,512]{1,0:T(8,128)(4,1)S(1)} %bitcast.43), kind=kLoop, calls=%fused_computation.27 | loop fusion | flops 6291456 | bytes 25174016 | tf_op jit(solution)/shard_map/jit(_where)/select_n | solution.py:68
  126.5 6.6 all-to-all-done.2
  146.8 188.7 %all-to-all-done.1 = bf16[16,512,768]{2,1,0:T(8,128)(2,1)} async-done(((bf16[16,512,768]{2,1,0:T(8,128)(2,1)}), bf16[16,512,768]{2,1,0:T(8,128)(2,1)}, u32[]{:S(2)}, u32[]{:S(2)}) %all-to-all-start.1) | async-done | bytes 12582944 | tf_op jit(solution)/shard_map/all_to_all | solution.py:75
  335.5 11.2 %fusion.20 = bf16[8192,768]{1,0:T(8,128)(2,1)} fusion(bf16[16,512,768]{2,1,0:T(8,128)(2,1)} %all-to-all-done.1, f32[16,2,768]{2,1,0:T(2,128)S(1)} %reshape.154), kind=kLoop, calls=%fused_computation.23 | loop fusion | flops 18874368 | bytes 25264128 | tf_op jit(solution)/shard_map/convert_element_type | solution.py:85
  346.8 17.7 %broadcast_select_fusion = (bf16[8192,768]{1,0:T(8,128)(2,1)}, bf16[8192,768]{1,0:T(8,128)(2,1)}) fusion(pred[8192]{0:T(1024)(128)(4,1)S(1)} %broadcast_in_dim.78, bf16[8192,768]{1,0:T(8,128)(2,1)} %fusion.20, bf16[768,768]{1,0:T(8,128)(2,1)S(1)} %copy-done), kind=kOutput, calls=%fused_computation.26 | convolution fusion | flops 9676259328 | bytes 38936576 | tf_op jit(solution)/shard_map/dot_general | solution.py:86
  364.5 405.9 %while.13 = (s32[]{:T(128)}, f32[256,768]{0,1:T(8,128)S(1)}, f32[256,96]{1,0:T(8,128)S(1)}, s32[16]{0:T(128)S(1)}, bf16[8192,768]{1,0:T(8,128)(2,1)}, /*index=5*...) while((s32[]{:T(128)}, f32[256,768]{0,1:T(8,128)S(1)}, ...), condition=%wide.region_6.7_spmd.clone, body=%wide.region_5.6_spmd.clone.sunk | while | flops 277266432 | bytes 6883518 | solution.py:41
  368.3 10.8 %fusion.47 = f32[256,768]{0,1:T(8,128)S(1)} fusion(s32[512,96]{0,1:T(8,128)S(1)} %constant_dynamic-slice_fusion.6, pred[512]{0:T(512)(128)(4,1)S(1)} %dynamic_slice.26, bf16[512,768]{0,1:T(8,128)(2,1)S(1)} %copy.40, f32[256,768]{0,1:T(8,128)S(1)} %get-tuple-element.188, pred[]{:T(512)S(6)} %compare.5), kind=kOutput, calls=%fused_computation.15.clone.2 | convolution fusion | flops 226885632 | bytes 2556417 | tf_op jit(solution)/shard_map/while/body/eval_jaxpr/rmk,rme->kme/dot_general | solution.py:32
  379.1 10.7 %fusion.48 = f32[1,96,256]{2,0,1:T(1,128)S(1)} fusion(s32[512,96]{0,1:T(8,128)S(1)} %constant_dynamic-slice_fusion.6, pred[512]{0:T(512)(128)(4,1)S(1)} %dynamic_slice.26), kind=kOutput, calls=%fused_computation.8.clone.3 | convolution fusion | flops 50331648 | bytes 295424 | tf_op jit(solution)/shard_map/while/body/eval_jaxpr/rmk,r->km/dot_general | solution.py:35
  393.6 10.8 %fusion.47 = f32[256,768]{0,1:T(8,128)S(1)} fusion(s32[512,96]{0,1:T(8,128)S(1)} %constant_dynamic-slice_fusion.6, pred[512]{0:T(512)(128)(4,1)S(1)} %dynamic_slice.26, bf16[512,768]{0,1:T(8,128)(2,1)S(1)} %copy.40, f32[256,768]{0,1:T(8,128)S(1)} %get-tuple-element.188, pred[]{:T(512)S(6)} %compare.5), kind=kOutput, calls=%fused_computation.15.clone.2 | convolution fusion | flops 226885632 | bytes 2556417 | tf_op jit(solution)/shard_map/while/body/eval_jaxpr/rmk,rme->kme/dot_general | solution.py:32
  404.4 10.7 %fusion.48 = f32[1,96,256]{2,0,1:T(1,128)S(1)} fusion(s32[512,96]{0,1:T(8,128)S(1)} %constant_dynamic-slice_fusion.6, pred[512]{0:T(512)(128)(4,1)S(1)} %dynamic_slice.26), kind=kOutput, calls=%fused_computation.8.clone.3 | convolution fusion | flops 50331648 | bytes 295424 | tf_op jit(solution)/shard_map/while/body/eval_jaxpr/rmk,r->km/dot_general | solution.py:35
  419.0 10.8 %fusion.47 = f32[256,768]{0,1:T(8,128)S(1)} fusion(s32[512,96]{0,1:T(8,128)S(1)} %constant_dynamic-slice_fusion.6, pred[512]{0:T(512)(128)(4,1)S(1)} %dynamic_slice.26, bf16[512,768]{0,1:T(8,128)(2,1)S(1)} %copy.40, f32[256,768]{0,1:T(8,128)S(1)} %get-tuple-element.188, pred[]{:T(512)S(6)} %compare.5), kind=kOutput, calls=%fused_computation.15.clone.2 | convolution fusion | flops 226885632 | bytes 2556417 | tf_op jit(solution)/shard_map/while/body/eval_jaxpr/rmk,rme->kme/dot_general | solution.py:32
  429.8 10.7 %fusion.48 = f32[1,96,256]{2,0,1:T(1,128)S(1)} fusion(s32[512,96]{0,1:T(8,128)S(1)} %constant_dynamic-slice_fusion.6, pred[512]{0:T(512)(128)(4,1)S(1)} %dynamic_slice.26), kind=kOutput, calls=%fused_computation.8.clone.3 | convolution fusion | flops 50331648 | bytes 295424 | tf_op jit(solution)/shard_map/while/body/eval_jaxpr/rmk,r->km/dot_general | solution.py:35
  444.4 10.8 %fusion.47 = f32[256,768]{0,1:T(8,128)S(1)} fusion(s32[512,96]{0,1:T(8,128)S(1)} %constant_dynamic-slice_fusion.6, pred[512]{0:T(512)(128)(4,1)S(1)} %dynamic_slice.26, bf16[512,768]{0,1:T(8,128)(2,1)S(1)} %copy.40, f32[256,768]{0,1:T(8,128)S(1)} %get-tuple-element.188, pred[]{:T(512)S(6)} %compare.5), kind=kOutput, calls=%fused_computation.15.clone.2 | convolution fusion | flops 226885632 | bytes 2556417 | tf_op jit(solution)/shard_map/while/body/eval_jaxpr/rmk,rme->kme/dot_general | solution.py:32
  455.2 10.7 %fusion.48 = f32[1,96,256]{2,0,1:T(1,128)S(1)} fusion(s32[512,96]{0,1:T(8,128)S(1)} %constant_dynamic-slice_fusion.6, pred[512]{0:T(512)(128)(4,1)S(1)} %dynamic_slice.26), kind=kOutput, calls=%fused_computation.8.clone.3 | convolution fusion | flops 50331648 | bytes 295424 | tf_op jit(solution)/shard_map/while/body/eval_jaxpr/rmk,r->km/dot_general | solution.py:35
  469.7 10.8 %fusion.47 = f32[256,768]{0,1:T(8,128)S(1)} fusion(s32[512,96]{0,1:T(8,128)S(1)} %constant_dynamic-slice_fusion.6, pred[512]{0:T(512)(128)(4,1)S(1)} %dynamic_slice.26, bf16[512,768]{0,1:T(8,128)(2,1)S(1)} %copy.40, f32[256,768]{0,1:T(8,128)S(1)} %get-tuple-element.188, pred[]{:T(512)S(6)} %compare.5), kind=kOutput, calls=%fused_computation.15.clone.2 | convolution fusion | flops 226885632 | bytes 2556417 | tf_op jit(solution)/shard_map/while/body/eval_jaxpr/rmk,rme->kme/dot_general | solution.py:32
  480.5 10.7 %fusion.48 = f32[1,96,256]{2,0,1:T(1,128)S(1)} fusion(s32[512,96]{0,1:T(8,128)S(1)} %constant_dynamic-slice_fusion.6, pred[512]{0:T(512)(128)(4,1)S(1)} %dynamic_slice.26), kind=kOutput, calls=%fused_computation.8.clone.3 | convolution fusion | flops 50331648 | bytes 295424 | tf_op jit(solution)/shard_map/while/body/eval_jaxpr/rmk,r->km/dot_general | solution.py:35
  495.1 10.8 %fusion.47 = f32[256,768]{0,1:T(8,128)S(1)} fusion(s32[512,96]{0,1:T(8,128)S(1)} %constant_dynamic-slice_fusion.6, pred[512]{0:T(512)(128)(4,1)S(1)} %dynamic_slice.26, bf16[512,768]{0,1:T(8,128)(2,1)S(1)} %copy.40, f32[256,768]{0,1:T(8,128)S(1)} %get-tuple-element.188, pred[]{:T(512)S(6)} %compare.5), kind=kOutput, calls=%fused_computation.15.clone.2 | convolution fusion | flops 226885632 | bytes 2556417 | tf_op jit(solution)/shard_map/while/body/eval_jaxpr/rmk,rme->kme/dot_general | solution.py:32
  505.9 10.7 %fusion.48 = f32[1,96,256]{2,0,1:T(1,128)S(1)} fusion(s32[512,96]{0,1:T(8,128)S(1)} %constant_dynamic-slice_fusion.6, pred[512]{0:T(512)(128)(4,1)S(1)} %dynamic_slice.26), kind=kOutput, calls=%fused_computation.8.clone.3 | convolution fusion | flops 50331648 | bytes 295424 | tf_op jit(solution)/shard_map/while/body/eval_jaxpr/rmk,r->km/dot_general | solution.py:35
  520.5 10.8 %fusion.47 = f32[256,768]{0,1:T(8,128)S(1)} fusion(s32[512,96]{0,1:T(8,128)S(1)} %constant_dynamic-slice_fusion.6, pred[512]{0:T(512)(128)(4,1)S(1)} %dynamic_slice.26, bf16[512,768]{0,1:T(8,128)(2,1)S(1)} %copy.40, f32[256,768]{0,1:T(8,128)S(1)} %get-tuple-element.188, pred[]{:T(512)S(6)} %compare.5), kind=kOutput, calls=%fused_computation.15.clone.2 | convolution fusion | flops 226885632 | bytes 2556417 | tf_op jit(solution)/shard_map/while/body/eval_jaxpr/rmk,rme->kme/dot_general | solution.py:32
  531.3 10.7 %fusion.48 = f32[1,96,256]{2,0,1:T(1,128)S(1)} fusion(s32[512,96]{0,1:T(8,128)S(1)} %constant_dynamic-slice_fusion.6, pred[512]{0:T(512)(128)(4,1)S(1)} %dynamic_slice.26), kind=kOutput, calls=%fused_computation.8.clone.3 | convolution fusion | flops 50331648 | bytes 295424 | tf_op jit(solution)/shard_map/while/body/eval_jaxpr/rmk,r->km/dot_general | solution.py:35
  545.8 10.8 %fusion.47 = f32[256,768]{0,1:T(8,128)S(1)} fusion(s32[512,96]{0,1:T(8,128)S(1)} %constant_dynamic-slice_fusion.6, pred[512]{0:T(512)(128)(4,1)S(1)} %dynamic_slice.26, bf16[512,768]{0,1:T(8,128)(2,1)S(1)} %copy.40, f32[256,768]{0,1:T(8,128)S(1)} %get-tuple-element.188, pred[]{:T(512)S(6)} %compare.5), kind=kOutput, calls=%fused_computation.15.clone.2 | convolution fusion | flops 226885632 | bytes 2556417 | tf_op jit(solution)/shard_map/while/body/eval_jaxpr/rmk,rme->kme/dot_general | solution.py:32
  556.6 10.7 %fusion.48 = f32[1,96,256]{2,0,1:T(1,128)S(1)} fusion(s32[512,96]{0,1:T(8,128)S(1)} %constant_dynamic-slice_fusion.6, pred[512]{0:T(512)(128)(4,1)S(1)} %dynamic_slice.26), kind=kOutput, calls=%fused_computation.8.clone.3 | convolution fusion | flops 50331648 | bytes 295424 | tf_op jit(solution)/shard_map/while/body/eval_jaxpr/rmk,r->km/dot_general | solution.py:35
  571.2 10.8 %fusion.47 = f32[256,768]{0,1:T(8,128)S(1)} fusion(s32[512,96]{0,1:T(8,128)S(1)} %constant_dynamic-slice_fusion.6, pred[512]{0:T(512)(128)(4,1)S(1)} %dynamic_slice.26, bf16[512,768]{0,1:T(8,128)(2,1)S(1)} %copy.40, f32[256,768]{0,1:T(8,128)S(1)} %get-tuple-element.188, pred[]{:T(512)S(6)} %compare.5), kind=kOutput, calls=%fused_computation.15.clone.2 | convolution fusion | flops 226885632 | bytes 2556417 | tf_op jit(solution)/shard_map/while/body/eval_jaxpr/rmk,rme->kme/dot_general | solution.py:32
  582.0 10.7 %fusion.48 = f32[1,96,256]{2,0,1:T(1,128)S(1)} fusion(s32[512,96]{0,1:T(8,128)S(1)} %constant_dynamic-slice_fusion.6, pred[512]{0:T(512)(128)(4,1)S(1)} %dynamic_slice.26), kind=kOutput, calls=%fused_computation.8.clone.3 | convolution fusion | flops 50331648 | bytes 295424 | tf_op jit(solution)/shard_map/while/body/eval_jaxpr/rmk,r->km/dot_general | solution.py:35
  596.6 10.8 %fusion.47 = f32[256,768]{0,1:T(8,128)S(1)} fusion(s32[512,96]{0,1:T(8,128)S(1)} %constant_dynamic-slice_fusion.6, pred[512]{0:T(512)(128)(4,1)S(1)} %dynamic_slice.26, bf16[512,768]{0,1:T(8,128)(2,1)S(1)} %copy.40, f32[256,768]{0,1:T(8,128)S(1)} %get-tuple-element.188, pred[]{:T(512)S(6)} %compare.5), kind=kOutput, calls=%fused_computation.15.clone.2 | convolution fusion | flops 226885632 | bytes 2556417 | tf_op jit(solution)/shard_map/while/body/eval_jaxpr/rmk,rme->kme/dot_general | solution.py:32
  607.4 10.7 %fusion.48 = f32[1,96,256]{2,0,1:T(1,128)S(1)} fusion(s32[512,96]{0,1:T(8,128)S(1)} %constant_dynamic-slice_fusion.6, pred[512]{0:T(512)(128)(4,1)S(1)} %dynamic_slice.26), kind=kOutput, calls=%fused_computation.8.clone.3 | convolution fusion | flops 50331648 | bytes 295424 | tf_op jit(solution)/shard_map/while/body/eval_jaxpr/rmk,r->km/dot_general | solution.py:35
  621.9 10.8 %fusion.47 = f32[256,768]{0,1:T(8,128)S(1)} fusion(s32[512,96]{0,1:T(8,128)S(1)} %constant_dynamic-slice_fusion.6, pred[512]{0:T(512)(128)(4,1)S(1)} %dynamic_slice.26, bf16[512,768]{0,1:T(8,128)(2,1)S(1)} %copy.40, f32[256,768]{0,1:T(8,128)S(1)} %get-tuple-element.188, pred[]{:T(512)S(6)} %compare.5), kind=kOutput, calls=%fused_computation.15.clone.2 | convolution fusion | flops 226885632 | bytes 2556417 | tf_op jit(solution)/shard_map/while/body/eval_jaxpr/rmk,rme->kme/dot_general | solution.py:32
  632.7 10.7 %fusion.48 = f32[1,96,256]{2,0,1:T(1,128)S(1)} fusion(s32[512,96]{0,1:T(8,128)S(1)} %constant_dynamic-slice_fusion.6, pred[512]{0:T(512)(128)(4,1)S(1)} %dynamic_slice.26), kind=kOutput, calls=%fused_computation.8.clone.3 | convolution fusion | flops 50331648 | bytes 295424 | tf_op jit(solution)/shard_map/while/body/eval_jaxpr/rmk,r->km/dot_general | solution.py:35
  647.3 10.8 %fusion.47 = f32[256,768]{0,1:T(8,128)S(1)} fusion(s32[512,96]{0,1:T(8,128)S(1)} %constant_dynamic-slice_fusion.6, pred[512]{0:T(512)(128)(4,1)S(1)} %dynamic_slice.26, bf16[512,768]{0,1:T(8,128)(2,1)S(1)} %copy.40, f32[256,768]{0,1:T(8,128)S(1)} %get-tuple-element.188, pred[]{:T(512)S(6)} %compare.5), kind=kOutput, calls=%fused_computation.15.clone.2 | convolution fusion | flops 226885632 | bytes 2556417 | tf_op jit(solution)/shard_map/while/body/eval_jaxpr/rmk,rme->kme/dot_general | solution.py:32
  658.1 10.7 %fusion.48 = f32[1,96,256]{2,0,1:T(1,128)S(1)} fusion(s32[512,96]{0,1:T(8,128)S(1)} %constant_dynamic-slice_fusion.6, pred[512]{0:T(512)(128)(4,1)S(1)} %dynamic_slice.26), kind=kOutput, calls=%fused_computation.8.clone.3 | convolution fusion | flops 50331648 | bytes 295424 | tf_op jit(solution)/shard_map/while/body/eval_jaxpr/rmk,r->km/dot_general | solution.py:35
  672.7 10.8 %fusion.47 = f32[256,768]{0,1:T(8,128)S(1)} fusion(s32[512,96]{0,1:T(8,128)S(1)} %constant_dynamic-slice_fusion.6, pred[512]{0:T(512)(128)(4,1)S(1)} %dynamic_slice.26, bf16[512,768]{0,1:T(8,128)(2,1)S(1)} %copy.40, f32[256,768]{0,1:T(8,128)S(1)} %get-tuple-element.188, pred[]{:T(512)S(6)} %compare.5), kind=kOutput, calls=%fused_computation.15.clone.2 | convolution fusion | flops 226885632 | bytes 2556417 | tf_op jit(solution)/shard_map/while/body/eval_jaxpr/rmk,rme->kme/dot_general | solution.py:32
  683.5 10.7 %fusion.48 = f32[1,96,256]{2,0,1:T(1,128)S(1)} fusion(s32[512,96]{0,1:T(8,128)S(1)} %constant_dynamic-slice_fusion.6, pred[512]{0:T(512)(128)(4,1)S(1)} %dynamic_slice.26), kind=kOutput, calls=%fused_computation.8.clone.3 | convolution fusion | flops 50331648 | bytes 295424 | tf_op jit(solution)/shard_map/while/body/eval_jaxpr/rmk,r->km/dot_general | solution.py:35
  698.0 10.8 %fusion.47 = f32[256,768]{0,1:T(8,128)S(1)} fusion(s32[512,96]{0,1:T(8,128)S(1)} %constant_dynamic-slice_fusion.6, pred[512]{0:T(512)(128)(4,1)S(1)} %dynamic_slice.26, bf16[512,768]{0,1:T(8,128)(2,1)S(1)} %copy.40, f32[256,768]{0,1:T(8,128)S(1)} %get-tuple-element.188, pred[]{:T(512)S(6)} %compare.5), kind=kOutput, calls=%fused_computation.15.clone.2 | convolution fusion | flops 226885632 | bytes 2556417 | tf_op jit(solution)/shard_map/while/body/eval_jaxpr/rmk,rme->kme/dot_general | solution.py:32
  708.8 10.7 %fusion.48 = f32[1,96,256]{2,0,1:T(1,128)S(1)} fusion(s32[512,96]{0,1:T(8,128)S(1)} %constant_dynamic-slice_fusion.6, pred[512]{0:T(512)(128)(4,1)S(1)} %dynamic_slice.26), kind=kOutput, calls=%fused_computation.8.clone.3 | convolution fusion | flops 50331648 | bytes 295424 | tf_op jit(solution)/shard_map/while/body/eval_jaxpr/rmk,r->km/dot_general | solution.py:35
  723.4 10.8 %fusion.47 = f32[256,768]{0,1:T(8,128)S(1)} fusion(s32[512,96]{0,1:T(8,128)S(1)} %constant_dynamic-slice_fusion.6, pred[512]{0:T(512)(128)(4,1)S(1)} %dynamic_slice.26, bf16[512,768]{0,1:T(8,128)(2,1)S(1)} %copy.40, f32[256,768]{0,1:T(8,128)S(1)} %get-tuple-element.188, pred[]{:T(512)S(6)} %compare.5), kind=kOutput, calls=%fused_computation.15.clone.2 | convolution fusion | flops 226885632 | bytes 2556417 | tf_op jit(solution)/shard_map/while/body/eval_jaxpr/rmk,rme->kme/dot_general | solution.py:32
  734.2 10.7 %fusion.48 = f32[1,96,256]{2,0,1:T(1,128)S(1)} fusion(s32[512,96]{0,1:T(8,128)S(1)} %constant_dynamic-slice_fusion.6, pred[512]{0:T(512)(128)(4,1)S(1)} %dynamic_slice.26), kind=kOutput, calls=%fused_computation.8.clone.3 | convolution fusion | flops 50331648 | bytes 295424 | tf_op jit(solution)/shard_map/while/body/eval_jaxpr/rmk,r->km/dot_general | solution.py:35
  748.8 10.8 %fusion.47 = f32[256,768]{0,1:T(8,128)S(1)} fusion(s32[512,96]{0,1:T(8,128)S(1)} %constant_dynamic-slice_fusion.6, pred[512]{0:T(512)(128)(4,1)S(1)} %dynamic_slice.26, bf16[512,768]{0,1:T(8,128)(2,1)S(1)} %copy.40, f32[256,768]{0,1:T(8,128)S(1)} %get-tuple-element.188, pred[]{:T(512)S(6)} %compare.5), kind=kOutput, calls=%fused_computation.15.clone.2 | convolution fusion | flops 226885632 | bytes 2556417 | tf_op jit(solution)/shard_map/while/body/eval_jaxpr/rmk,rme->kme/dot_general | solution.py:32
  759.6 10.7 %fusion.48 = f32[1,96,256]{2,0,1:T(1,128)S(1)} fusion(s32[512,96]{0,1:T(8,128)S(1)} %constant_dynamic-slice_fusion.6, pred[512]{0:T(512)(128)(4,1)S(1)} %dynamic_slice.26), kind=kOutput, calls=%fused_computation.8.clone.3 | convolution fusion | flops 50331648 | bytes 295424 | tf_op jit(solution)/shard_map/while/body/eval_jaxpr/rmk,r->km/dot_general | solution.py:35
  771.6 150.6 %all-reduce.5.cloned.1.call-done = (f32[256,768]{1,0:T(8,128)}, f32[256,96]{1,0:T(8,128)}) async-done(((f32[256,768]{1,0:T(8,128)}, f32[256,96]{1,0:T(8,128)}), (f32[256,768]{1,0:T(8,128)}, f32[256,96]{1,0:T(8,128)})) %all-reduce.5.cloned.1.call-update) | async-done | bytes 884752
  (161 shorter events, 89.2 us)
Async XLA Ops:
  7.2 339.6 %copy-start = (bf16[768,768]{1,0:T(8,128)(2,1)S(1)}, bf16[768,768]{1,0:T(8,128)(2,1)}, u32[]{:S(2)}) copy-start(bf16[768,768]{1,0:T(8,128)(2,1)} %param.13) | copy-start | bytes 3538948
  10.5 72.4 %all-to-all-start = ((s32[16,1,2]{2,1,0:T(1,128)}), s32[16,1,2]{2,1,0:T(1,128)S(1)}, u32[]{:S(2)}, u32[]{:S(2)}) async-start(s32[16,1,2]{2,1,0:T(1,128)} %bitcast.3), calls=%async_computation | async-start | bytes 16384 | tf_op jit(solution)/shard_map/all_to_all | solution.py:78
  31.0 15.0 %copy-start.3 = (s32[3072,96]{0,1:T(8,128)S(1)}, s32[3072,96]{0,1:T(8,128)}, u32[]{:S(2)}) copy-start(s32[3072,96]{0,1:T(8,128)} %param.10) | copy-start | bytes 3538948
  82.9 50.1 %all-to-all-start.2 = ((s32[16,512,96]{1,2,0:T(8,128)}), s32[16,512,96]{1,2,0:T(8,128)}, u32[]{:S(2)}, u32[]{:S(2)}) async-start(s32[16,512,96]{1,2,0:T(8,128)} %copy.30), calls=%async_computation.2 | async-start | bytes 6291456 | tf_op jit(solution)/shard_map/all_to_all | solution.py:77
  133.0 202.5 %all-to-all-start.1 = ((bf16[16,512,768]{2,1,0:T(8,128)(2,1)}), bf16[16,512,768]{2,1,0:T(8,128)(2,1)}, u32[]{:S(2)}, u32[]{:S(2)}) async-start(bf16[16,512,768]{2,1,0:T(8,128)(2,1)} %broadcast_select_fusion.1), calls=%async_computation.1 | async-start | bytes 25165824 | tf_op jit(solution)/shard_map/all_to_all | solution.py:75
  138.0 784.2 %all-reduce.5.cloned.1.call-start = ((), (), s32[]{:S(2)}) async-start(), calls=%async_computation.3 | async-start | bytes 1835008
  770.4 1.2 copy-start.2
  770.4 154.4 %copy-start.1 = (bf16[768,768]{1,0:T(8,128)(2,1)S(1)}, bf16[768,768]{1,0:T(8,128)(2,1)}, u32[]{:S(2)}) copy-start(bf16[768,768]{1,0:T(8,128)(2,1)} %param.13) | copy-start | bytes 3538948
Sparse Core Ops, SparseCore 0:
  771.7 150.4 all-reduce.4
where the time goes:
time: 945 us; the launch traced here: 932 us
  matrix products  361 us (38%)
  waiting for transfers between devices  346 us (37%)
  local copies, waits for them, and re-layouts  136 us (14%)
  other arithmetic  43.1 us (5%)
  starting transfers between devices  20.6 us (2%)
  between operations  14.6 us (2%)
  loops' own time  11.5 us (1%)
    all_to_all x1, waiting for transfers between devices, shards(): lax.all_to_all(outgoing, 'list', split_axis=0, concat_axis=0, tiled=True)  189 us
    dot_general x16, matrix products, accumulate(): jnp.einsum('rmk,rme->kme', selector, rows_here, preferred_element_type=jn...  173 us
    dot_general x16, matrix products, accumulate(): jnp.einsum('rmk,r->km', selector, ones_column, preferred_element_type=jnp...  170 us
    unnamed x2, waiting for transfers between devices  151 us
    gather x4, local copies, waits for them, and re-layouts, shards(): vector_blocks[source_block]  47.4 us
    dynamic_slice x32, local copies, waits for them, and re-layouts, accumulate(): lax.dynamic_slice_in_dim(encoded, start, step_rows, 0)  23.4 us
  transfers between devices with their start and end apart: 4, of which 3 were waited for; matrix products, arithmetic and copies ran while one was open for 12% of the time, Pallas kernels for 0%

commit v1 on v0

v1 whole, which is shorter than its diff:
```python
import jax
import jax.numpy as jnp
from jax import lax
from jax.experimental import pallas as pl
from jax.experimental.pallas import tpu as pltpu
from jax.sharding import PartitionSpec as P

M = 96
D = 768
KS = 256
LIST_DEV = 4096
BLK = 256
BDEV = 12
ROWS_DEV = BDEV * BLK
N_LIST = 16
N_INGEST = 8
LANES = 128
CHUNKS = D // LANES
WIDE = D + LANES
HI = 64
MESH = pl.DeviceIdType.MESH
F32 = jnp.float32
BF16 = jnp.bfloat16
FAR = (1, 3, 2)


def iota(shape, axis):
    return lax.broadcasted_iota(jnp.int32, shape, axis)


def exchange(
    vec_hbm, lists, codes_hbm, counts, cent_hbm, rot_hbm,
    stored, mid, share,
    vec, codes, cent, rot, stage, landed, ids_out, ids_in, ids_smem, centre_rows, rows_in, table,
    natural, left, right, left_c, right_c, totals, ring_in, ring_sum, part_out, part_in,
    load_sem, smem_sem, s1, r1, s2, r2, out_sem, s_ids, r_ids, s_rows, r_rows, s_ring, r_ring, s_part, r_part,
):
    i = lax.axis_index("ingest")
    j = lax.axis_index("list")
    y = j // 4
    z = j % 4

    def at(dy, dz):
        return ((y + dy) % 4) * 4 + (z + dz) % 4

    loads = [
        pltpu.make_async_copy(vec_hbm, vec, load_sem.at[0]),
        pltpu.make_async_copy(cent_hbm, cent, load_sem.at[1]),
        pltpu.make_async_copy(codes_hbm, codes, load_sem.at[2]),
        pltpu.make_async_copy(rot_hbm, rot, load_sem.at[3]),
    ]
    for load in loads:
        load.start()

    barrier = pltpu.get_barrier_semaphore()
    for o in range(1, N_LIST):
        pl.semaphore_signal(barrier, inc=1, device_id=(i, at(o // 4, o % 4)), device_id_type=MESH)
    for o in range(1, N_INGEST):
        pl.semaphore_signal(barrier, inc=1, device_id=((i + o) % N_INGEST, j), device_id_type=MESH)

    owners = [lists[b] >> 12 for b in range(BDEV)]
    slots = []
    for b in range(BDEV):
        rank = jnp.int32(0)
        for c in range(b):
            rank = rank + jnp.where(owners[c] == owners[b], 1, 0)
        limit = jnp.int32(0)
        for o in range(N_LIST):
            limit = jnp.where(owners[b] == o, counts[0, o], limit)
        slots.append(jnp.where(rank < limit, owners[b] * 2 + rank, -1))
    for b in range(BDEV):
        table[b] = slots[b]

    def source_of(slot):
        block = jnp.int32(0)
        for b in range(1, BDEV):
            block = jnp.where(slots[b] == slot, b, block)
        return block

    def list_of(slot):
        found = jnp.int32(-1)
        for b in range(BDEV):
            found = jnp.where(slots[b] == slot, lists[b] & (LIST_DEV - 1), found)
        return found

    lane8 = iota((8, LANES), 1)
    for o in range(N_LIST):
        owner = at(o // 4, o % 4)
        ids_out[o] = jnp.where(lane8 == 0, list_of(owner * 2), list_of(owner * 2 + 1))
    ids_in[j] = ids_out[0]

    pl.semaphore_wait(barrier, N_LIST - 1 + N_INGEST - 1)

    id_copies = []
    for o in range(1, N_LIST):
        copy = pltpu.make_async_remote_copy(
            src_ref=ids_out.at[o], dst_ref=ids_in.at[j], send_sem=s_ids.at[o], recv_sem=r_ids.at[o],
            device_id=(i, at(o // 4, o % 4)), device_id_type=MESH)
        copy.start()
        id_copies.append(copy)

    loads[0].wait()

    first = {}
    place = 0
    for d in FAR:
        for e in range(4):
            for r in range(2):
                owner = at(e, d) if r == 0 else at(d, e)
                hop = at(0, d) if r == 0 else at(d, 0)
                stage[place] = vec[source_of(owner * 2 + r)]
                if e == 0:
                    copy = pltpu.make_async_remote_copy(
                        src_ref=stage.at[place], dst_ref=landed.at[j * 2 + r], send_sem=s2.at[r, d, 0],
                        recv_sem=r2.at[r, d, 0], device_id=(i, hop), device_id_type=MESH)
                else:
                    copy = pltpu.make_async_remote_copy(
                        src_ref=stage.at[place], dst_ref=mid.at[r, d, e], send_sem=s1.at[r, d, e],
                        recv_sem=r1.at[r, d, e], device_id=(i, hop), device_id_type=MESH)
                copy.start()
                first[r, d, e] = copy
                place += 1

    second = []
    for e in FAR:
        for r in range(2):
            owner = at(e, 0) if r == 0 else at(0, e)
            stage[place] = vec[source_of(owner * 2 + r)]
            copy = pltpu.make_async_remote_copy(
                src_ref=stage.at[place], dst_ref=landed.at[j * 2 + r], send_sem=s2.at[r, 0, e], recv_sem=r2.at[r, 0, e],
                device_id=(i, owner), device_id_type=MESH)
            copy.start()
            second.append(copy)
            place += 1
    for r in range(2):
        landed[j * 2 + r] = vec[source_of(j * 2 + r)]

    for copy in id_copies:
        copy.wait_recv()
    to_smem = pltpu.make_async_copy(ids_in, ids_smem, smem_sem.at[0])
    to_smem.start()
    to_smem.wait()
    loads[1].wait()
    sub16 = iota((16, D), 0)
    pad = jnp.zeros((2, LANES), F32)
    row_copies = []
    for o in range(N_LIST):
        source = at(-(o // 4) % 4, -(o % 4) % 4)
        parts = []
        for r in range(2):
            wanted = jnp.maximum(ids_smem[source, 0, r], 0)
            near = cent[wanted >> 4].astype(F32)
            row = jnp.sum(jnp.where(sub16 == (wanted & 15), near, 0.0), axis=0, keepdims=True)
            parts += [row[:, k * LANES:(k + 1) * LANES] for k in range(CHUNKS)] + [pad]
        centre_rows[source] = jnp.concatenate(parts, axis=0).astype(BF16)
        if o == 0:
            rows_in[j] = centre_rows[source]
        else:
            copy = pltpu.make_async_remote_copy(
                src_ref=centre_rows.at[source], dst_ref=rows_in.at[j], send_sem=s_rows.at[o], recv_sem=r_rows.at[o],
                device_id=(i, source), device_id_type=MESH)
            copy.start()
            row_copies.append(copy)
    loads[2].wait()
    loads[3].wait()
    for copy in row_copies:
        copy.wait_recv()

    eye = (iota((BLK, BLK), 0) == iota((BLK, BLK), 1)).astype(BF16)
    none = jnp.zeros((LANES - M, BLK), F32)

    def rotate(rows, centre):
        residual = jnp.concatenate([
            (rows[:, k * LANES:(k + 1) * LANES].astype(F32) - centre[k:k + 1, :]).astype(BF16) for k in range(CHUNKS)
        ], axis=1)
        return jnp.dot(residual, rot[...], preferred_element_type=F32)

    def encode(b, carry):
        slot = table[b]
        kept = slot >= 0
        slot = jnp.maximum(slot, 0)
        tile = rows_in[slot >> 1].astype(F32)
        centre = jnp.where((slot & 1) == 0, tile[0:8], tile[8:16])
        vec[b] = jnp.where(kept, rotate(vec[b], centre), 0.0).astype(BF16)
        code = codes[:, pl.ds(pl.multiple_of(b * BLK, BLK), BLK)]
        both = jnp.concatenate([
            (code >> 6).astype(F32), none, jnp.where(kept, (code >> 4).astype(F32), -1.0), none], axis=0).astype(BF16)
        natural[b] = lax.dot_general(
            eye, both, (((1,), (1,)), ((), ())), preferred_element_type=F32).astype(BF16)
        return carry

    lax.fori_loop(0, BDEV, encode, 0)

    totals[:, D:] = jnp.zeros((KS, LANES), F32)
    lane = iota((BLK, LANES), 1)
    upper = (lane >= 64).astype(F32)
    lane_r = iota((HI, 2 * LANES), 1)
    lane_c = iota((HI, LANES), 1)
    lane_16 = iota((16, 2 * LANES), 1)
    hi_rows = iota((HI, BLK), 0)
    wide_row = iota((LANES, 2 * LANES), 0)
    wide_lane = iota((LANES, 2 * LANES), 1)
    digit = (iota((BLK, 2 * LANES), 1) // 16).astype(F32)

    def group(g, carry):
        spread = (wide_row == g * 16 + (wide_lane // LANES) * 8 + (wide_lane % 64) // 8).astype(BF16)
        spread_c = (wide_row == g * 16 + wide_lane % 16).astype(BF16)
        cols = pl.ds(pl.multiple_of(g * LANES, LANES), LANES)
        base = pl.multiple_of(g * 16, 16)

        def build(b, inner):
            rows = pl.ds(pl.multiple_of(b * BLK, BLK), BLK)
            lo = jnp.dot(natural[b, :, :LANES], spread, preferred_element_type=F32)
            e = vec[b, :, cols].astype(F32)
            turned = pltpu.roll(e, 64, 1)
            for h in range(2):
                both = jnp.where(lane < 64, e, turned) if h == 0 else jnp.where(lane < 64, turned, e)
                lo_h = lo[:, h * LANES:(h + 1) * LANES]
                for p in range(2):
                    right[h, rows, p * LANES:(p + 1) * LANES] = jnp.where(
                        lo_h == upper + float(2 * p), both, 0.0).astype(BF16)
            high = jnp.dot(natural[b, :, LANES:], spread_c, preferred_element_type=F32)
            right_c[rows, :] = jnp.where(high == digit, 1.0, 0.0).astype(BF16)
            code = codes[pl.ds(base, 16), rows] & 15
            for m in range(16):
                left_c[m * 16:(m + 1) * 16, rows] = jnp.where(
                    code[m:m + 1, :] == hi_rows[:16], 1.0, 0.0).astype(BF16)
            return inner

        lax.fori_loop(0, BDEV, build, 0)
        halves = []
        for h in range(2):

            def build_left(b, inner):
                rows = pl.ds(pl.multiple_of(b * BLK, BLK), BLK)
                code = codes[pl.ds(base + h * 8, 8), rows] & (HI - 1)
                for m in range(8):
                    left[m * HI:(m + 1) * HI, rows] = jnp.where(code[m:m + 1, :] == hi_rows, 1.0, 0.0).astype(BF16)
                return inner

            lax.fori_loop(0, BDEV, build_left, 0)
            sums = jnp.dot(left[...], right[h], preferred_element_type=F32)
            picked = jnp.zeros((HI, 2 * LANES), F32)
            for m in range(8):
                picked = picked + jnp.where((lane_r % 64) // 8 == m, sums[m * HI:(m + 1) * HI, :], 0.0)
            halves.append(picked)
        for p in range(2):
            a = halves[0][:, p * LANES:(p + 1) * LANES]
            c = halves[1][:, p * LANES:(p + 1) * LANES]
            totals[(2 * p) * HI:(2 * p + 1) * HI, cols] = jnp.where(lane_c < 64, a, pltpu.roll(c, 64, 1))
            totals[(2 * p + 1) * HI:(2 * p + 2) * HI, cols] = jnp.where(lane_c < 64, pltpu.roll(a, 64, 1), c)
        found = jnp.dot(left_c[...], right_c[...], preferred_element_type=F32)
        picked = jnp.zeros((16, 2 * LANES), F32)
        for m in range(16):
            picked = picked + jnp.where(lane_16 % 16 == m, found[m * 16:(m + 1) * 16, :], 0.0)
        for q in range(16):
            part = picked[:, (q // 8) * LANES:(q // 8 + 1) * LANES]
            moved = pltpu.roll(part, (g * 16 - (q % 8) * 16) % LANES, 1)
            totals[q * 16:(q + 1) * 16, D:] += jnp.where(lane_c[:16] // 16 == g, moved, 0.0)
        return carry

    lax.fori_loop(0, CHUNKS, group, 0)

    slab = KS // N_INGEST
    ring_copies = []
    for o in range(1, N_INGEST):
        target = (i + o) % N_INGEST
        copy = pltpu.make_async_remote_copy(
            src_ref=totals.at[pl.ds(pl.multiple_of(target * slab, slab), slab), :], dst_ref=ring_in.at[o],
            send_sem=s_ring.at[o], recv_sem=r_ring.at[o], device_id=(target, j), device_id_type=MESH)
        copy.start()
        ring_copies.append(copy)

    for d in FAR:
        for e in FAR:
            for r in range(2):
                owner = at(e, 0) if r == 0 else at(0, e)
                origin = at(0, -d) if r == 0 else at(-d, 0)
                first[r, d, e].wait_recv()
                copy = pltpu.make_async_remote_copy(
                    src_ref=mid.at[r, d, e], dst_ref=landed.at[origin * 2 + r], send_sem=s2.at[r, d, e],
                    recv_sem=r2.at[r, d, e], device_id=(i, owner), device_id_type=MESH)
                copy.start()
                second.append(copy)

    for copy in ring_copies:
        copy.wait_recv()
    whole = totals[pl.ds(pl.multiple_of(i * slab, slab), slab), :]
    for o in range(1, N_INGEST):
        whole = whole + ring_in[o]
    ring_sum[...] = whole
    zero_row = jnp.zeros((1, LANES), F32)
    for o in range(N_LIST):
        target = at(o // 4, o % 4)
        eight = ring_sum[pl.ds(pl.multiple_of((target // 4) * 8, 8), 8), :]
        rows = []
        for r in range(2):
            row = jnp.sum(jnp.where(iota((8, WIDE), 0) == (target % 4) * 2 + r, eight, 0.0), axis=0, keepdims=True)
            rows += [row[:, k * LANES:(k + 1) * LANES] for k in range(CHUNKS + 1)] + [zero_row]
        part_out[o] = jnp.concatenate(rows, axis=0)
    part_copies = []
    for o in range(1, N_LIST):
        copy = pltpu.make_async_remote_copy(
            src_ref=part_out.at[o], dst_ref=part_in.at[o], send_sem=s_part.at[o], recv_sem=r_part.at[o],
            device_id=(i, at(o // 4, o % 4)), device_id_type=MESH)
        copy.start()
        part_copies.append(copy)

    def write_of(slot):
        return pltpu.make_async_copy(landed.at[slot], stored.at[slot], out_sem.at[slot])

    def finish(slot, r):
        source = slot // 2
        centre = centre_rows[source].astype(F32)[r * 8:(r + 1) * 8]
        rotated = rotate(landed[slot], centre)
        landed[slot] = jnp.where(ids_smem[source, 0, r] >= 0, rotated, 0.0).astype(BF16)
        write_of(slot).start()

    def arrival(d, e):
        for r in range(2):
            origin = at(4 - e, 4 - d) if r == 0 else at(4 - d, 4 - e)
            slot = origin * 2 + r
            pltpu.make_async_remote_copy(
                src_ref=stage.at[0], dst_ref=landed.at[slot], send_sem=s2.at[r, d, e], recv_sem=r2.at[r, d, e],
                device_id=(i, origin), device_id_type=MESH).wait_recv()
            finish(slot, r)

    for r in range(2):
        finish(j * 2 + r, r)

    def near_first(t, carry):
        arrival(t + 1, 0)
        return carry

    def near_second(t, carry):
        arrival(0, t + 1)
        return carry

    def far(t, carry):
        arrival(t // 3 + 1, t % 3 + 1)
        return carry

    lax.fori_loop(0, 3, near_first, 0)
    lax.fori_loop(0, 3, near_second, 0)
    for copy in part_copies:
        copy.wait_recv()
    total = part_out[0]
    for o in range(1, N_LIST):
        total = total + part_in[o]
    share[...] = total
    lax.fori_loop(0, 9, far, 0)

    for copy in id_copies + row_copies + ring_copies + part_copies + list(first.values()) + second:
        copy.wait_send()

    def written(slot, carry):
        write_of(slot).wait()
        return carry

    lax.fori_loop(0, 2 * N_LIST, written, 0)


def shards(vectors, list_ids, code_ids, block_counts, centroids, rotation):
    hbm = pl.BlockSpec(memory_space=pl.ANY)
    smem = pl.BlockSpec(memory_space=pltpu.SMEM)
    vmem = pl.BlockSpec(memory_space=pltpu.VMEM)
    dma = pltpu.SemaphoreType.DMA
    stored, _, share = pl.pallas_call(
        exchange,
        out_shape=(
            jax.ShapeDtypeStruct((2 * N_LIST, BLK, D), BF16),
            jax.ShapeDtypeStruct((2, 4, 4, BLK, D), BF16),
            jax.ShapeDtypeStruct((16, LANES), F32),
        ),
        in_specs=[hbm, smem, hbm, smem, hbm, hbm],
        out_specs=(hbm, hbm, vmem),
        scratch_shapes=[
            pltpu.VMEM((BDEV, BLK, D), BF16),
            pltpu.VMEM((M, ROWS_DEV), jnp.int32),
            pltpu.VMEM((LIST_DEV // 16, 16, D), BF16),
            pltpu.VMEM((D, D), BF16),
            pltpu.VMEM((2 * N_LIST - 2, BLK, D), BF16),
            pltpu.VMEM((2 * N_LIST, BLK, D), BF16),
            pltpu.VMEM((N_LIST, 8, LANES), jnp.int32),
            pltpu.VMEM((N_LIST, 8, LANES), jnp.int32),
            pltpu.SMEM((N_LIST, 8, LANES), jnp.int32),
            pltpu.VMEM((N_LIST, 16, LANES), BF16),
            pltpu.VMEM((N_LIST, 16, LANES), BF16),
            pltpu.SMEM((BDEV,), jnp.int32),
            pltpu.VMEM((BDEV, BLK, 2 * LANES), BF16),
            pltpu.VMEM((8 * HI, ROWS_DEV), BF16),
            pltpu.VMEM((2, ROWS_DEV, 2 * LANES), BF16),
            pltpu.VMEM((2 * LANES, ROWS_DEV), BF16),
            pltpu.VMEM((ROWS_DEV, 2 * LANES), BF16),
            pltpu.VMEM((KS, WIDE), F32),
            pltpu.VMEM((N_INGEST, KS // N_INGEST, WIDE), F32),
            pltpu.VMEM((KS // N_INGEST, WIDE), F32),
            pltpu.VMEM((N_LIST, 16, LANES), F32),
            pltpu.VMEM((N_LIST, 16, LANES), F32),
            dma((4,)), dma((1,)),
            dma((2, 4, 4)), dma((2, 4, 4)), dma((2, 4, 4)), dma((2, 4, 4)), dma((2 * N_LIST,)),
            dma((N_LIST,)), dma((N_LIST,)), dma((N_LIST,)), dma((N_LIST,)),
            dma((N_INGEST,)), dma((N_INGEST,)), dma((N_LIST,)), dma((N_LIST,)),
        ],
        compiler_params=pltpu.CompilerParams(
            collective_id=1, has_side_effects=True, vmem_limit_bytes=62 * 1024 * 1024),
        name="exchange",
    )(
        vectors.reshape(BDEV, BLK, D), list_ids, code_ids.T, block_counts,
        centroids.reshape(LIST_DEV // 16, 16, D), rotation,
    )
    parts = share.reshape(2, 8, LANES)
    return stored.reshape(2 * N_LIST * BLK, D), parts[:, :CHUNKS].reshape(2, D), parts[:, CHUNKS, :M]


def solution(mesh):
    both = ("ingest", "list")
    in_specs = (P(both, None), P(both), P(both, None), P(both, None), P("list", None), P())
    out_specs = (P(both, None), P(both, None), P(both, None))
    return jax.shard_map(shards, mesh=mesh, in_specs=in_specs, out_specs=out_specs, check_vma=False)
```

time: 945 us -> 234 us (0.25); the launches traced: 932 us -> 234 us
  matrix products: 361 us -> 0 us
  waiting for transfers between devices: 346 us -> 0 us
  Pallas kernels: 0 us -> 220 us
  local copies, waits for them, and re-layouts: 136 us -> 13 us
  other arithmetic: 43.1 us -> 0 us
  starting transfers between devices: 20.6 us -> 0 us
  between operations: 14.6 us -> 0.64 us
  loops' own time: 11.5 us -> 0 us
    dot_general x33 -> x0, matrix products: 361 us -> none  [the longest x16 173 us: accumulate(): jnp.einsum('rmk,rme->kme', selector, rows_here, preferred_element_type=jn...]
    pallas_call x0 -> x1, Pallas kernels: none -> 220 us  [shards(): pl.pallas_call(exchange, out_shape=(jax.ShapeDtypeStruct((2 * N_LIST, BLK...]
    all_to_all x3 -> x0, waiting for transfers between devices: 195 us -> none  [the longest x1 189 us: shards(): lax.all_to_all(outgoing, 'list', split_axis=0, concat_axis=0, tiled=True)]
    unnamed x2 -> x0, waiting for transfers between devices: 151 us -> none
    gather x8 -> x0, local copies, waits for them, and re-layouts: 60 us -> none  [the longest x4 47.4 us: shards(): vector_blocks[source_block]]
    dynamic_slice x80 -> x0, local copies, waits for them, and re-layouts: 49.3 us -> none  [the longest x32 23.4 us: accumulate(): lax.dynamic_slice_in_dim(encoded, start, step_rows, 0)]
    all_to_all x3 -> x0, starting transfers between devices: 20.5 us -> none  [the longest x1 8.13 us: shards(): lax.all_to_all(outgoing_lists, 'list', split_axis=0, concat_axis=0, tiled...]
    select_n x4 -> x0, other arithmetic: 16.1 us -> none  [the longest x1 10.9 us: shards(): jnp.where(filled[:, None], vector_blocks[source_block], jnp.zeros((), jnp...]
  transfers between devices with their start and end apart: 4 -> 0, of which waited for: 3 -> 0; matrix products, arithmetic and copies ran while one was open for 12% -> 0% of each run, Pallas kernels for 0% -> 0%
where the time goes in v1:
time: 234 us
  Pallas kernels  220 us (94%)
  local copies, waits for them, and re-layouts  13 us (6%)
    pallas_call x1, Pallas kernels, shards(): pl.pallas_call(exchange, out_shape=(jax.ShapeDtypeStruct((2 * N_LIST, BLK...  220 us
    unnamed x3, local copies, waits for them, and re-layouts  11.7 us

profile of v1, /device:TPU:0, one launch (start us, length us, event | category | flops | bytes accessed | tf_op | source)
XLA Modules:
  0.0 233.9 jit_solution(13602718207980333281)
XLA Ops:
  0.6 220.2 %exchange.1 = (bf16[32,256,768]{2,1,0:T(8,128)(2,1)}, bf16[2,4,4,256,768]{4,3,2,1,0:T(8,128)(2,1)}, f32[16,128]{1,0:T(8,128)}) custom-call(bf16[12,256,768]{2,1,0:T(8,128)(2,1)} %bitcast.15, s32[12]{0:T(128)} %lists.1, s32[96,3072]{1,0:T(8,128)} %bitcast.16, s32[1,16]{1,0:T(1,128)} %counts.1, bf16[256,16,768]{2,1,0:T(8,128)(2,1)} %bitcast.14, ...), custom_call_target="tpu_custom_call" | custom-call | tf_op jit(solution)/shard_map/exchange/pallas_call | solution.py:368
  220.9 1.3 slice.9
  222.1 0.7 slice_bitcast_fusion
  222.8 0.6 copy.14
  223.4 10.5 %copy.16 = bf16[8192,768]{1,0:T(8,128)(2,1)} copy(bf16[8192,768]{1,0:T(8,128)(2,1)} %bitcast.13) | data formatting | bytes 25165824

commit v2 on v1

--- a/solution.py
+++ b/solution.py
@@ -24,16 +24,19 @@
 FAR = (1, 3, 2)
 
 
+ORDER = [(d, e, r) for e in (1, 3, 2, 0) for d in (1, 3, 2) for r in range(2)]
+
+
 def iota(shape, axis):
     return lax.broadcasted_iota(jnp.int32, shape, axis)
 
 
 def exchange(
     vec_hbm, lists, codes_hbm, counts, cent_hbm, rot_hbm,
-    stored, mid, share,
-    vec, codes, cent, rot, stage, landed, ids_out, ids_in, ids_smem, centre_rows, rows_in, table,
+    landed, mid, share,
+    vec, codes, cent, rot, stage, ids_out, ids_in, ids_smem, centre_rows, rows_in, table,
     natural, left, right, left_c, right_c, totals, ring_in, ring_sum, part_out, part_in,
-    load_sem, smem_sem, s1, r1, s2, r2, out_sem, s_ids, r_ids, s_rows, r_rows, s_ring, r_ring, s_part, r_part,
+    load_sem, smem_sem, s1, r1, s2, r2, s_ids, r_ids, s_rows, r_rows, s_ring, r_ring, s_part, r_part,
 ):
     i = lax.axis_index("ingest")
     j = lax.axis_index("list")
@@ -49,8 +52,7 @@
         pltpu.make_async_copy(codes_hbm, codes, load_sem.at[2]),
         pltpu.make_async_copy(rot_hbm, rot, load_sem.at[3]),
     ]
-    for load in loads:
-        load.start()
+    loads[0].start()
 
     barrier = pltpu.get_barrier_semaphore()
     for o in range(1, N_LIST):
@@ -99,13 +101,15 @@
         copy.start()
         id_copies.append(copy)
 
+    for load in loads[1:]:
+        load.start()
     loads[0].wait()
 
     first = {}
     place = 0
-    for d in FAR:
-        for e in range(4):
-            for r in range(2):
+    for d, e, r in ORDER[:4]:
+        if True:
+            if True:
                 owner = at(e, d) if r == 0 else at(d, e)
                 hop = at(0, d) if r == 0 else at(d, 0)
                 stage[place] = vec[source_of(owner * 2 + r)]
@@ -120,20 +124,6 @@
                 copy.start()
                 first[r, d, e] = copy
                 place += 1
-
-    second = []
-    for e in FAR:
-        for r in range(2):
-            owner = at(e, 0) if r == 0 else at(0, e)
-            stage[place] = vec[source_of(owner * 2 + r)]
-            copy = pltpu.make_async_remote_copy(
-                src_ref=stage.at[place], dst_ref=landed.at[j * 2 + r], send_sem=s2.at[r, 0, e], recv_sem=r2.at[r, 0, e],
-                device_id=(i, owner), device_id_type=MESH)
-            copy.start()
-            second.append(copy)
-            place += 1
-    for r in range(2):
-        landed[j * 2 + r] = vec[source_of(j * 2 + r)]
 
     for copy in id_copies:
         copy.wait_recv()
@@ -161,6 +151,38 @@
                 device_id=(i, source), device_id_type=MESH)
             copy.start()
             row_copies.append(copy)
+    for d, e, r in ORDER[4:]:
+        if True:
+            if True:
+                owner = at(e, d) if r == 0 else at(d, e)
+                hop = at(0, d) if r == 0 else at(d, 0)
+                stage[place] = vec[source_of(owner * 2 + r)]
+                if e == 0:
+                    copy = pltpu.make_async_remote_copy(
+                        src_ref=stage.at[place], dst_ref=landed.at[j * 2 + r], send_sem=s2.at[r, d, 0],
+                        recv_sem=r2.at[r, d, 0], device_id=(i, hop), device_id_type=MESH)
+                else:
+                    copy = pltpu.make_async_remote_copy(
+                        src_ref=stage.at[place], dst_ref=mid.at[r, d, e], send_sem=s1.at[r, d, e],
+                        recv_sem=r1.at[r, d, e], device_id=(i, hop), device_id_type=MESH)
+                copy.start()
+                first[r, d, e] = copy
+                place += 1
+
+    second = []
+    for e in FAR:
+        for r in range(2):
+            owner = at(e, 0) if r == 0 else at(0, e)
+            stage[place] = vec[source_of(owner * 2 + r)]
+            copy = pltpu.make_async_remote_copy(
+                src_ref=stage.at[place], dst_ref=landed.at[j * 2 + r], send_sem=s2.at[r, 0, e], recv_sem=r2.at[r, 0, e],
+                device_id=(i, owner), device_id_type=MESH)
+            copy.start()
+            second.append(copy)
+            place += 1
+    for r in range(2):
+        landed[j * 2 + r] = vec[source_of(j * 2 + r)]
+
     loads[2].wait()
     loads[3].wait()
     for copy in row_copies:
@@ -306,15 +328,11 @@
         copy.start()
         part_copies.append(copy)
 
-    def write_of(slot):
-        return pltpu.make_async_copy(landed.at[slot], stored.at[slot], out_sem.at[slot])
-
     def finish(slot, r):
         source = slot // 2
         centre = centre_rows[source].astype(F32)[r * 8:(r + 1) * 8]
         rotated = rotate(landed[slot], centre)
         landed[slot] = jnp.where(ids_smem[source, 0, r] >= 0, rotated, 0.0).astype(BF16)
-        write_of(slot).start()
 
     def arrival(d, e):
         for r in range(2):
@@ -337,7 +355,7 @@
         return carry
 
     def far(t, carry):
-        arrival(t // 3 + 1, t % 3 + 1)
+        arrival((t // 3 * 2) % 3 + 1, (t % 3 * 2) % 3 + 1)
         return carry
 
     lax.fori_loop(0, 3, near_first, 0)
@@ -353,11 +371,15 @@
     for copy in id_copies + row_copies + ring_copies + part_copies + list(first.values()) + second:
         copy.wait_send()
 
-    def written(slot, carry):
-        write_of(slot).wait()
-        return carry
-
-    lax.fori_loop(0, 2 * N_LIST, written, 0)
+
+def deliver(landed, share, stored, sums, counts, sem):
+    whole = pltpu.make_async_copy(landed, stored, sem.at[0])
+    whole.start()
+    for r in range(2):
+        for k in range(CHUNKS):
+            sums[r:r + 1, k * LANES:(k + 1) * LANES] = share[r * 8 + k:r * 8 + k + 1, :]
+        counts[r:r + 1, :] = share[r * 8 + CHUNKS:r * 8 + CHUNKS + 1, :M]
+    whole.wait()
 
 
 def shards(vectors, list_ids, code_ids, block_counts, centroids, rotation):
@@ -365,22 +387,21 @@
     smem = pl.BlockSpec(memory_space=pltpu.SMEM)
     vmem = pl.BlockSpec(memory_space=pltpu.VMEM)
     dma = pltpu.SemaphoreType.DMA
-    stored, _, share = pl.pallas_call(
+    landed, _, share = pl.pallas_call(
         exchange,
         out_shape=(
-            jax.ShapeDtypeStruct((2 * N_LIST, BLK, D), BF16),
+            pltpu.VMEM((2 * N_LIST, BLK, D), BF16),
             jax.ShapeDtypeStruct((2, 4, 4, BLK, D), BF16),
-            jax.ShapeDtypeStruct((16, LANES), F32),
+            pltpu.VMEM((16, LANES), F32),
         ),
         in_specs=[hbm, smem, hbm, smem, hbm, hbm],
-        out_specs=(hbm, hbm, vmem),
+        out_specs=(vmem, hbm, vmem),
         scratch_shapes=[
             pltpu.VMEM((BDEV, BLK, D), BF16),
             pltpu.VMEM((M, ROWS_DEV), jnp.int32),
             pltpu.VMEM((LIST_DEV // 16, 16, D), BF16),
             pltpu.VMEM((D, D), BF16),
             pltpu.VMEM((2 * N_LIST - 2, BLK, D), BF16),
-            pltpu.VMEM((2 * N_LIST, BLK, D), BF16),
             pltpu.VMEM((N_LIST, 8, LANES), jnp.int32),
             pltpu.VMEM((N_LIST, 8, LANES), jnp.int32),
             pltpu.SMEM((N_LIST, 8, LANES), jnp.int32),
@@ -398,19 +419,31 @@
             pltpu.VMEM((N_LIST, 16, LANES), F32),
             pltpu.VMEM((N_LIST, 16, LANES), F32),
             dma((4,)), dma((1,)),
-            dma((2, 4, 4)), dma((2, 4, 4)), dma((2, 4, 4)), dma((2, 4, 4)), dma((2 * N_LIST,)),
+            dma((2, 4, 4)), dma((2, 4, 4)), dma((2, 4, 4)), dma((2, 4, 4)),
             dma((N_LIST,)), dma((N_LIST,)), dma((N_LIST,)), dma((N_LIST,)),
             dma((N_INGEST,)), dma((N_INGEST,)), dma((N_LIST,)), dma((N_LIST,)),
         ],
         compiler_params=pltpu.CompilerParams(
-            collective_id=1, has_side_effects=True, vmem_limit_bytes=62 * 1024 * 1024),
+            collective_id=1, has_side_effects=True, vmem_limit_bytes=47 * 1024 * 1024),
         name="exchange",
     )(
         vectors.reshape(BDEV, BLK, D), list_ids, code_ids.T, block_counts,
         centroids.reshape(LIST_DEV // 16, 16, D), rotation,
     )
-    parts = share.reshape(2, 8, LANES)
-    return stored.reshape(2 * N_LIST * BLK, D), parts[:, :CHUNKS].reshape(2, D), parts[:, CHUNKS, :M]
+    stored, sums, counts = pl.pallas_call(
+        deliver,
+        out_shape=(
+            jax.ShapeDtypeStruct((2 * N_LIST, BLK, D), BF16),
+            jax.ShapeDtypeStruct((2, D), F32),
+            jax.ShapeDtypeStruct((2, M), F32),
+        ),
+        in_specs=[vmem, vmem],
+        out_specs=(hbm, vmem, vmem),
+        scratch_shapes=[dma((1,))],
+        compiler_params=pltpu.CompilerParams(vmem_limit_bytes=16 * 1024 * 1024),
+        name="deliver",
+    )(landed, share)
+    return stored.reshape(2 * N_LIST * BLK, D), sums, counts
 
 
 def solution(mesh):

time: 234 us -> 169 us (0.72)
  Pallas kernels: 220 us -> 168 us
  local copies, waits for them, and re-layouts: 13 us -> 0 us
    pallas_call x1 -> x2, Pallas kernels: 220 us -> 168 us  [the longest x1 162 us: shards(): pl.pallas_call(exchange, out_shape=(pltpu.VMEM((2 * N_LIST, BLK, D), BF16...]
    unnamed x3 -> x0, local copies, waits for them, and re-layouts: 11.7 us -> none
where the time goes in v2:
time: 169 us
  Pallas kernels  168 us (99%)
    pallas_call x1, Pallas kernels, shards(): pl.pallas_call(exchange, out_shape=(pltpu.VMEM((2 * N_LIST, BLK, D), BF16...  162 us
    pallas_call x1, Pallas kernels, shards(): pl.pallas_call(deliver, out_shape=(jax.ShapeDtypeStruct((2 * N_LIST, BLK,...  5.38 us

profile of v2, /device:TPU:0, one launch (start us, length us, event | category | flops | bytes accessed | tf_op | source)
XLA Modules:
  0.0 168.5 jit_solution(1684691641064046492)
XLA Ops:
  0.6 162.5 %exchange.1 = (bf16[32,256,768]{2,1,0:T(8,128)(2,1)S(1)}, bf16[2,4,4,256,768]{4,3,2,1,0:T(8,128)(2,1)}, f32[16,128]{1,0:T(8,128)S(1)}) custom-call(bf16[12,256,768]{2,1,0:T(8,128)(2,1)} %bitcast.5, s32[12]{0:T(128)} %lists.1, s32[96,3072]{1,0:T(8,128)} %bitcast.6, s32[1,16]{1,0:T(1,128)} %counts.1, bf16[256,16,768]{2,1,0:T(8,128)(2,1)} %bitcast.4, ...), custom_call_target="tpu_custom_call" | custom-call | tf_op jit(solution)/shard_map/exchange/pallas_call | solution.py:390
  163.1 5.4 %deliver.1 = (bf16[32,256,768]{2,1,0:T(8,128)(2,1)}, f32[2,768]{1,0:T(2,128)}, f32[2,96]{1,0:T(2,128)}) custom-call(bf16[32,256,768]{2,1,0:T(8,128)(2,1)S(1)} %get-tuple-element.8.landed, f32[16,128]{1,0:T(8,128)S(1)} %get-tuple-element.9.share), custom_call_target="tpu_custom_call" | custom-call | tf_op jit(solution)/shard_map/deliver/pallas_call | solution.py:433

commit v3 on v2

--- a/solution.py
+++ b/solution.py
@@ -24,7 +24,9 @@
 FAR = (1, 3, 2)
 
 
-ORDER = [(d, e, r) for e in (1, 3, 2, 0) for d in (1, 3, 2) for r in range(2)]
+RAW = ((1, 1), (3, 1), (1, 3), (3, 3))
+LATER = ((2, 1), (2, 3), (1, 2), (3, 2), (2, 2))
+LAST = ((1, 0), (3, 0), (2, 0), (0, 1), (0, 3), (0, 2))
 
 
 def iota(shape, axis):
@@ -105,25 +107,32 @@
         load.start()
     loads[0].wait()
 
-    first = {}
-    place = 0
-    for d, e, r in ORDER[:4]:
-        if True:
-            if True:
-                owner = at(e, d) if r == 0 else at(d, e)
-                hop = at(0, d) if r == 0 else at(d, 0)
-                stage[place] = vec[source_of(owner * 2 + r)]
-                if e == 0:
-                    copy = pltpu.make_async_remote_copy(
-                        src_ref=stage.at[place], dst_ref=landed.at[j * 2 + r], send_sem=s2.at[r, d, 0],
-                        recv_sem=r2.at[r, d, 0], device_id=(i, hop), device_id_type=MESH)
-                else:
-                    copy = pltpu.make_async_remote_copy(
-                        src_ref=stage.at[place], dst_ref=mid.at[r, d, e], send_sem=s1.at[r, d, e],
-                        recv_sem=r1.at[r, d, e], device_id=(i, hop), device_id_type=MESH)
-                copy.start()
-                first[r, d, e] = copy
-                place += 1
+    hops = {}
+
+    def send(place, d, e, r, packed):
+        stage[place] = packed
+        along = (0, d) if r == 0 else (d, 0)
+        if d == 0:
+            along = (e, 0) if r == 0 else (0, e)
+        if d == 0 or e == 0:
+            landing, gone, come = landed.at[j * 2 + r], s2.at[r, d, e], r2.at[r, d, e]
+        else:
+            landing, gone, come = mid.at[r, d, e], s1.at[r, d, e], r1.at[r, d, e]
+        copy = pltpu.make_async_remote_copy(
+            src_ref=stage.at[place], dst_ref=landing, send_sem=gone, recv_sem=come,
+            device_id=(i, at(*along)), device_id_type=MESH)
+        copy.start()
+        hops[r, d, e] = copy
+
+    def slot_of(d, e, r):
+        return (at(e, d) if r == 0 else at(d, e)) * 2 + r
+
+    def send_raw(first, pairs):
+        for n, (d, e) in enumerate(pairs):
+            for r in range(2):
+                send(first + 2 * n + r, d, e, r, vec[source_of(slot_of(d, e, r))])
+
+    send_raw(0, RAW[:2])
 
     for copy in id_copies:
         copy.wait_recv()
@@ -151,38 +160,8 @@
                 device_id=(i, source), device_id_type=MESH)
             copy.start()
             row_copies.append(copy)
-    for d, e, r in ORDER[4:]:
-        if True:
-            if True:
-                owner = at(e, d) if r == 0 else at(d, e)
-                hop = at(0, d) if r == 0 else at(d, 0)
-                stage[place] = vec[source_of(owner * 2 + r)]
-                if e == 0:
-                    copy = pltpu.make_async_remote_copy(
-                        src_ref=stage.at[place], dst_ref=landed.at[j * 2 + r], send_sem=s2.at[r, d, 0],
-                        recv_sem=r2.at[r, d, 0], device_id=(i, hop), device_id_type=MESH)
-                else:
-                    copy = pltpu.make_async_remote_copy(
-                        src_ref=stage.at[place], dst_ref=mid.at[r, d, e], send_sem=s1.at[r, d, e],
-                        recv_sem=r1.at[r, d, e], device_id=(i, hop), device_id_type=MESH)
-                copy.start()
-                first[r, d, e] = copy
-                place += 1
-
-    second = []
-    for e in FAR:
-        for r in range(2):
-            owner = at(e, 0) if r == 0 else at(0, e)
-            stage[place] = vec[source_of(owner * 2 + r)]
-            copy = pltpu.make_async_remote_copy(
-                src_ref=stage.at[place], dst_ref=landed.at[j * 2 + r], send_sem=s2.at[r, 0, e], recv_sem=r2.at[r, 0, e],
-                device_id=(i, owner), device_id_type=MESH)
-            copy.start()
-            second.append(copy)
-            place += 1
-    for r in range(2):
-        landed[j * 2 + r] = vec[source_of(j * 2 + r)]
-
+
+    send_raw(4, RAW[2:])
     loads[2].wait()
     loads[3].wait()
     for copy in row_copies:
@@ -213,6 +192,20 @@
 
     lax.fori_loop(0, BDEV, encode, 0)
 
+    def encoded(slot):
+        filled = jnp.int32(0)
+        for b in range(BDEV):
+            filled = filled + jnp.where(slots[b] == slot, 1, 0)
+        return jnp.where(filled > 0, vec[source_of(slot)], jnp.zeros((BLK, D), BF16))
+
+    place = 8
+    for d, e in LATER + LAST:
+        for r in range(2):
+            send(place, d, e, r, encoded(slot_of(d, e, r)))
+            place += 1
+    for r in range(2):
+        landed[j * 2 + r] = encoded(j * 2 + r)
+
     totals[:, D:] = jnp.zeros((KS, LANES), F32)
     lane = iota((BLK, LANES), 1)
     upper = (lane >= 64).astype(F32)
@@ -224,7 +217,30 @@
     wide_lane = iota((LANES, 2 * LANES), 1)
     digit = (iota((BLK, 2 * LANES), 1) // 16).astype(F32)
 
+    second = {}
+    for d, e in RAW + LATER:
+        for r in range(2):
+            owner = at(e, 0) if r == 0 else at(0, e)
+            origin = at(0, -d) if r == 0 else at(-d, 0)
+            second[r, d, e] = pltpu.make_async_remote_copy(
+                src_ref=mid.at[r, d, e], dst_ref=landed.at[origin * 2 + r], send_sem=s2.at[r, d, e],
+                recv_sem=r2.at[r, d, e], device_id=(i, owner), device_id_type=MESH)
+
+    def forward(pairs):
+        for d, e in pairs:
+            for r in range(2):
+                hops[r, d, e].wait_recv()
+                second[r, d, e].start()
+
     def group(g, carry):
+        @pl.when(g == 1)
+        def early():
+            forward(RAW[:2])
+
+        @pl.when(g == 3)
+        def next():
+            forward(RAW[2:])
+
         spread = (wide_row == g * 16 + (wide_lane // LANES) * 8 + (wide_lane % 64) // 8).astype(BF16)
         spread_c = (wide_row == g * 16 + wide_lane % 16).astype(BF16)
         cols = pl.ds(pl.multiple_of(g * LANES, LANES), LANES)
@@ -293,17 +309,7 @@
         copy.start()
         ring_copies.append(copy)
 
-    for d in FAR:
-        for e in FAR:
-            for r in range(2):
-                owner = at(e, 0) if r == 0 else at(0, e)
-                origin = at(0, -d) if r == 0 else at(-d, 0)
-                first[r, d, e].wait_recv()
-                copy = pltpu.make_async_remote_copy(
-                    src_ref=mid.at[r, d, e], dst_ref=landed.at[origin * 2 + r], send_sem=s2.at[r, d, e],
-                    recv_sem=r2.at[r, d, e], device_id=(i, owner), device_id_type=MESH)
-                copy.start()
-                second.append(copy)
+    forward(LATER)
 
     for copy in ring_copies:
         copy.wait_recv()
@@ -334,7 +340,8 @@
         rotated = rotate(landed[slot], centre)
         landed[slot] = jnp.where(ids_smem[source, 0, r] >= 0, rotated, 0.0).astype(BF16)
 
-    def arrival(d, e):
+    def arrival(t, carry):
+        d, e = 1 + 2 * (t % 2), 1 + 2 * (t // 2)
         for r in range(2):
             origin = at(4 - e, 4 - d) if r == 0 else at(4 - d, 4 - e)
             slot = origin * 2 + r
@@ -342,44 +349,36 @@
                 src_ref=stage.at[0], dst_ref=landed.at[slot], send_sem=s2.at[r, d, e], recv_sem=r2.at[r, d, e],
                 device_id=(i, origin), device_id_type=MESH).wait_recv()
             finish(slot, r)
-
-    for r in range(2):
-        finish(j * 2 + r, r)
-
-    def near_first(t, carry):
-        arrival(t + 1, 0)
         return carry
 
-    def near_second(t, carry):
-        arrival(0, t + 1)
-        return carry
-
-    def far(t, carry):
-        arrival((t // 3 * 2) % 3 + 1, (t % 3 * 2) % 3 + 1)
-        return carry
-
-    lax.fori_loop(0, 3, near_first, 0)
-    lax.fori_loop(0, 3, near_second, 0)
+    lax.fori_loop(0, 4, arrival, 0)
+
     for copy in part_copies:
         copy.wait_recv()
     total = part_out[0]
     for o in range(1, N_LIST):
         total = total + part_in[o]
     share[...] = total
-    lax.fori_loop(0, 9, far, 0)
-
-    for copy in id_copies + row_copies + ring_copies + part_copies + list(first.values()) + second:
+
+    for d, e in LATER + LAST:
+        for r in range(2):
+            (hops[r, d, e] if d == 0 or e == 0 else second[r, d, e]).wait_recv()
+    for copy in id_copies + row_copies + ring_copies + part_copies + list(hops.values()) + list(second.values()):
         copy.wait_send()
 
 
 def deliver(landed, share, stored, sums, counts, sem):
-    whole = pltpu.make_async_copy(landed, stored, sem.at[0])
-    whole.start()
+    parts = [
+        pltpu.make_async_copy(landed.at[pl.ds(n * 4, 4)], stored.at[pl.ds(n * 4, 4)], sem.at[n]) for n in range(8)
+    ]
+    for part in parts:
+        part.start()
     for r in range(2):
         for k in range(CHUNKS):
             sums[r:r + 1, k * LANES:(k + 1) * LANES] = share[r * 8 + k:r * 8 + k + 1, :]
         counts[r:r + 1, :] = share[r * 8 + CHUNKS:r * 8 + CHUNKS + 1, :M]
-    whole.wait()
+    for part in parts:
+        part.wait()
 
 
 def shards(vectors, list_ids, code_ids, block_counts, centroids, rotation):
@@ -439,7 +438,7 @@
         ),
         in_specs=[vmem, vmem],
         out_specs=(hbm, vmem, vmem),
-        scratch_shapes=[dma((1,))],
+        scratch_shapes=[dma((8,))],
         compiler_params=pltpu.CompilerParams(vmem_limit_bytes=16 * 1024 * 1024),
         name="deliver",
     )(landed, share)

time: 169 us -> 158 us (0.935)
  Pallas kernels: 168 us -> 157 us
    pallas_call x1, Pallas kernels: 162 us -> 152 us  [shards(): pl.pallas_call(exchange, out_shape=(pltpu.VMEM((2 * N_LIST, BLK, D), BF16...]
where the time goes in v3:
time: 158 us
  Pallas kernels  157 us (99%)
    pallas_call x1, Pallas kernels, shards(): pl.pallas_call(exchange, out_shape=(pltpu.VMEM((2 * N_LIST, BLK, D), BF16...  152 us
    pallas_call x1, Pallas kernels, shards(): pl.pallas_call(deliver, out_shape=(jax.ShapeDtypeStruct((2 * N_LIST, BLK,...  5.25 us

profile of v3, /device:TPU:0, one launch (start us, length us, event | category | flops | bytes accessed | tf_op | source)
XLA Modules:
  0.0 157.8 jit_solution(16141302971043509837)
XLA Ops:
  0.6 151.9 %exchange.1 = (bf16[32,256,768]{2,1,0:T(8,128)(2,1)S(1)}, bf16[2,4,4,256,768]{4,3,2,1,0:T(8,128)(2,1)}, f32[16,128]{1,0:T(8,128)S(1)}) custom-call(bf16[12,256,768]{2,1,0:T(8,128)(2,1)} %bitcast.5, s32[12]{0:T(128)} %lists.1, s32[96,3072]{1,0:T(8,128)} %bitcast.6, s32[1,16]{1,0:T(1,128)} %counts.1, bf16[256,16,768]{2,1,0:T(8,128)(2,1)} %bitcast.4, ...), custom_call_target="tpu_custom_call" | custom-call | tf_op jit(solution)/shard_map/exchange/pallas_call | solution.py:389
  152.6 5.3 %deliver.1 = (bf16[32,256,768]{2,1,0:T(8,128)(2,1)}, f32[2,768]{1,0:T(2,128)}, f32[2,96]{1,0:T(2,128)}) custom-call(bf16[32,256,768]{2,1,0:T(8,128)(2,1)S(1)} %get-tuple-element.8.landed, f32[16,128]{1,0:T(8,128)S(1)} %get-tuple-element.9.share), custom_call_target="tpu_custom_call" | custom-call | tf_op jit(solution)/shard_map/deliver/pallas_call | solution.py:432

commit v4 on v3

--- a/solution.py
+++ b/solution.py
@@ -98,7 +98,7 @@
     id_copies = []
     for o in range(1, N_LIST):
         copy = pltpu.make_async_remote_copy(
-            src_ref=ids_out.at[o], dst_ref=ids_in.at[j], send_sem=s_ids.at[o], recv_sem=r_ids.at[o],
+            src_ref=ids_out.at[o, pl.ds(0, 1)], dst_ref=ids_in.at[j, pl.ds(0, 1)], send_sem=s_ids.at[o], recv_sem=r_ids.at[o],
             device_id=(i, at(o // 4, o % 4)), device_id_type=MESH)
         copy.start()
         id_copies.append(copy)
@@ -199,10 +199,12 @@
         return jnp.where(filled > 0, vec[source_of(slot)], jnp.zeros((BLK, D), BF16))
 
     place = 8
-    for d, e in LATER + LAST:
-        for r in range(2):
-            send(place, d, e, r, encoded(slot_of(d, e, r)))
-            place += 1
+    def send_encoded(first, pairs):
+        for n, (d, e) in enumerate(pairs):
+            for r in range(2):
+                send(first + 2 * n + r, d, e, r, encoded(slot_of(d, e, r)))
+
+    send_encoded(8, LATER)
     for r in range(2):
         landed[j * 2 + r] = encoded(j * 2 + r)
 
@@ -309,7 +311,7 @@
         copy.start()
         ring_copies.append(copy)
 
-    forward(LATER)
+    send_encoded(18, LAST)
 
     for copy in ring_copies:
         copy.wait_recv()
@@ -333,6 +335,8 @@
             device_id=(i, at(o // 4, o % 4)), device_id_type=MESH)
         copy.start()
         part_copies.append(copy)
+
+    forward(LATER)
 
     def finish(slot, r):
         source = slot // 2

time: 158 us -> 157 us (level)
  no operation moved by 1% of the time
where the time goes in v4:
time: 157 us
  Pallas kernels  156 us (99%)
    pallas_call x1, Pallas kernels, shards(): pl.pallas_call(exchange, out_shape=(pltpu.VMEM((2 * N_LIST, BLK, D), BF16...  151 us
    pallas_call x1, Pallas kernels, shards(): pl.pallas_call(deliver, out_shape=(jax.ShapeDtypeStruct((2 * N_LIST, BLK,...  5.25 us

profile of v4, /device:TPU:0, one launch (start us, length us, event | category | flops | bytes accessed | tf_op | source)
XLA Modules:
  0.0 156.6 jit_solution(13880765613142219359)
XLA Ops:
  0.6 150.7 %exchange.1 = (bf16[32,256,768]{2,1,0:T(8,128)(2,1)S(1)}, bf16[2,4,4,256,768]{4,3,2,1,0:T(8,128)(2,1)}, f32[16,128]{1,0:T(8,128)S(1)}) custom-call(bf16[12,256,768]{2,1,0:T(8,128)(2,1)} %bitcast.5, s32[12]{0:T(128)} %lists.1, s32[96,3072]{1,0:T(8,128)} %bitcast.6, s32[1,16]{1,0:T(1,128)} %counts.1, bf16[256,16,768]{2,1,0:T(8,128)(2,1)} %bitcast.4, ...), custom_call_target="tpu_custom_call" | custom-call | tf_op jit(solution)/shard_map/exchange/pallas_call | solution.py:393
  151.3 5.3 %deliver.1 = (bf16[32,256,768]{2,1,0:T(8,128)(2,1)}, f32[2,768]{1,0:T(2,128)}, f32[2,96]{1,0:T(2,128)}) custom-call(bf16[32,256,768]{2,1,0:T(8,128)(2,1)S(1)} %get-tuple-element.8.landed, f32[16,128]{1,0:T(8,128)S(1)} %get-tuple-element.9.share), custom_call_target="tpu_custom_call" | custom-call | tf_op jit(solution)/shard_map/deliver/pallas_call | solution.py:436

commit v5 on v4

--- a/solution.py
+++ b/solution.py
@@ -93,16 +93,6 @@
         ids_out[o] = jnp.where(lane8 == 0, list_of(owner * 2), list_of(owner * 2 + 1))
     ids_in[j] = ids_out[0]
 
-    pl.semaphore_wait(barrier, N_LIST - 1 + N_INGEST - 1)
-
-    id_copies = []
-    for o in range(1, N_LIST):
-        copy = pltpu.make_async_remote_copy(
-            src_ref=ids_out.at[o, pl.ds(0, 1)], dst_ref=ids_in.at[j, pl.ds(0, 1)], send_sem=s_ids.at[o], recv_sem=r_ids.at[o],
-            device_id=(i, at(o // 4, o % 4)), device_id_type=MESH)
-        copy.start()
-        id_copies.append(copy)
-
     for load in loads[1:]:
         load.start()
     loads[0].wait()
@@ -110,7 +100,8 @@
     hops = {}
 
     def send(place, d, e, r, packed):
-        stage[place] = packed
+        if packed is not None:
+            stage[place] = packed
         along = (0, d) if r == 0 else (d, 0)
         if d == 0:
             along = (e, 0) if r == 0 else (0, e)
@@ -127,10 +118,26 @@
     def slot_of(d, e, r):
         return (at(e, d) if r == 0 else at(d, e)) * 2 + r
 
+    def pack_raw(first, pairs):
+        for n, (d, e) in enumerate(pairs):
+            for r in range(2):
+                stage[first + 2 * n + r] = vec[source_of(slot_of(d, e, r))]
+
     def send_raw(first, pairs):
         for n, (d, e) in enumerate(pairs):
             for r in range(2):
-                send(first + 2 * n + r, d, e, r, vec[source_of(slot_of(d, e, r))])
+                send(first + 2 * n + r, d, e, r, None)
+
+    pack_raw(0, RAW)
+    pl.semaphore_wait(barrier, N_LIST - 1 + N_INGEST - 1)
+
+    id_copies = []
+    for o in range(1, N_LIST):
+        copy = pltpu.make_async_remote_copy(
+            src_ref=ids_out.at[o, pl.ds(0, 1)], dst_ref=ids_in.at[j, pl.ds(0, 1)], send_sem=s_ids.at[o], recv_sem=r_ids.at[o],
+            device_id=(i, at(o // 4, o % 4)), device_id_type=MESH)
+        copy.start()
+        id_copies.append(copy)
 
     send_raw(0, RAW[:2])
 

time: 157 us -> 157 us (level)
  no operation moved by 1% of the time
where the time goes in v5:
time: 157 us; the launch traced here: 156 us
  Pallas kernels  156 us (99%)
    pallas_call x1, Pallas kernels, shards(): pl.pallas_call(exchange, out_shape=(pltpu.VMEM((2 * N_LIST, BLK, D), BF16...  151 us
    pallas_call x1, Pallas kernels, shards(): pl.pallas_call(deliver, out_shape=(jax.ShapeDtypeStruct((2 * N_LIST, BLK,...  5.25 us

profile of v5, /device:TPU:0, one launch (start us, length us, event | category | flops | bytes accessed | tf_op | source)
XLA Modules:
  0.0 156.5 jit_solution(16016265336069495330)
XLA Ops:
  0.6 150.6 %exchange.1 = (bf16[32,256,768]{2,1,0:T(8,128)(2,1)S(1)}, bf16[2,4,4,256,768]{4,3,2,1,0:T(8,128)(2,1)}, f32[16,128]{1,0:T(8,128)S(1)}) custom-call(bf16[12,256,768]{2,1,0:T(8,128)(2,1)} %bitcast.5, s32[12]{0:T(128)} %lists.1, s32[96,3072]{1,0:T(8,128)} %bitcast.6, s32[1,16]{1,0:T(1,128)} %counts.1, bf16[256,16,768]{2,1,0:T(8,128)(2,1)} %bitcast.4, ...), custom_call_target="tpu_custom_call" | custom-call | tf_op jit(solution)/shard_map/exchange/pallas_call | solution.py:400
  151.2 5.3 %deliver.1 = (bf16[32,256,768]{2,1,0:T(8,128)(2,1)}, f32[2,768]{1,0:T(2,128)}, f32[2,96]{1,0:T(2,128)}) custom-call(bf16[32,256,768]{2,1,0:T(8,128)(2,1)S(1)} %get-tuple-element.8.landed, f32[16,128]{1,0:T(8,128)S(1)} %get-tuple-element.9.share), custom_call_target="tpu_custom_call" | custom-call | tf_op jit(solution)/shard_map/deliver/pallas_call | solution.py:443
